TPU v7x, 512 devices: a whole 4x4x16 slice. The times are simulated.
512 devices in a mesh: ctx: 64 (over y, z), head: 8 (over x, core).
Axes of the slice: x: 4, y: 4, z: 16, core: 2. Of those that a mesh axis runs over, the one named last changes fastest.
Arguments:
- queries: bfloat16 [32768, 4096], P('ctx', 'head'), may hold values from -6 to 6
- keys: bfloat16 [32768, 4096], P('ctx', 'head'), may hold values from -6 to 6
- values: bfloat16 [32768, 4096], P('ctx', 'head'), may hold values from -6 to 6
- gain: float32 [4096], P('head'), may hold values from 0.1 to 1.9
- out_grad: bfloat16 [32768, 4096], P('ctx', 'head'), may hold values from -6 to 6
Outputs:
- normed: bfloat16 [32768, 4096], P('ctx', 'head')
- query_grad: bfloat16 [32768, 4096], P('ctx', 'head')
- key_grad: bfloat16 [32768, 4096], P('ctx', 'head')
- value_grad: bfloat16 [32768, 4096], P('ctx', 'head')
All inputs are finite; a program needn't handle non-finite values.
Results may differ from a plain program's by a relative error of at most 0.0058.
Values sent between devices are 32-bit elements; how exact they have to be, the bound alone decides.
A program may use at most 64 MiB of HBM per device.

v0:
```python
import jax
import jax.numpy as jnp
from jax import lax
from jax.sharding import PartitionSpec as P

HD = 128
BLOCK = 512


def entering(value, axis, combine, identity, reverse):
    length, mine = (lax.axis_size(axis), lax.axis_index(axis))
    everything = lax.all_gather(value, axis)
    start = jnp.broadcast_to(jnp.asarray(identity, value.dtype), value.shape)

    def turn(k, before):
        at = length - 1 - k if reverse else k
        reached = at > mine if reverse else at < mine
        new = combine(before, everything[at])
        return jnp.where(reached, new, before)

    return lax.fori_loop(0, length, turn, start)


def add_states(earlier, later):
    return earlier + later


def body(queries, keys, values, gain, out_grad):
    rows, width = queries.shape
    heads = width // HD
    blocks = rows // BLOCK
    shape4 = (blocks, BLOCK, heads, HD)
    f32 = jnp.float32
    qb = queries.reshape(shape4)
    kb = keys.reshape(shape4)
    vb = values.reshape(shape4)
    causal = jnp.tril(jnp.ones((BLOCK, BLOCK), dtype=bool))
    local_kv = jnp.einsum("nshi,nshj->nhij", kb, vb, preferred_element_type=f32)
    own_total = jnp.sum(local_kv, axis=0)
    carried = entering(own_total, "ctx", add_states, jnp.zeros_like(own_total), False)
    inner = jnp.concatenate([jnp.zeros_like(local_kv), jnp.cumsum(local_kv, axis=0)[:-1]], axis=0)
    states = (carried[None] + inner).astype(jnp.bfloat16)
    scores = jnp.where(
        causal, jnp.einsum("nthi,nshi->nhts", qb, kb, preferred_element_type=f32), 0.0
    )
    scores = scores.astype(jnp.bfloat16)
    attended = jnp.einsum("nhts,nshj->nthj", scores, vb, preferred_element_type=f32)
    attended = attended + jnp.einsum("nthi,nhij->nthj", qb, states, preferred_element_type=f32)
    gains = gain.reshape(heads, HD)
    upstream = gains * out_grad.reshape(shape4).astype(f32)
    ssq_local = jnp.sum(attended * attended, axis=(2, 3))
    mdot_local = jnp.sum(attended * upstream, axis=(2, 3))
    ssq, mdot = lax.psum((ssq_local, mdot_local), "head")
    features = width * lax.axis_size("head")
    rinv = lax.rsqrt(ssq / features + 1e-06)[:, :, None, None]
    normed = (attended * rinv * gains).astype(jnp.bfloat16).reshape(rows, width)
    d_att = (rinv * upstream - attended * rinv**3 * mdot[:, :, None, None] / features).astype(
        jnp.bfloat16
    )
    query_dot = jnp.einsum("nthi,nthj->nhij", qb, d_att, preferred_element_type=f32)
    dot_total = jnp.sum(query_dot, axis=0)
    later = entering(dot_total, "ctx", add_states, jnp.zeros_like(dot_total), True)
    inner_later = jnp.concatenate(
        [jnp.cumsum(query_dot[::-1], axis=0)[::-1][1:], jnp.zeros_like(query_dot)], axis=0
    )
    adjoint = (later[None] + inner_later).astype(jnp.bfloat16)
    back = jnp.where(
        causal, jnp.einsum("nthj,nshj->nhts", d_att, vb, preferred_element_type=f32), 0.0
    )
    back = back.astype(jnp.bfloat16)
    grad_q = jnp.einsum("nhts,nshi->nthi", back, kb, preferred_element_type=f32)
    grad_q = grad_q + jnp.einsum("nthj,nhij->nthi", d_att, states, preferred_element_type=f32)
    grad_k = jnp.einsum("nhts,nthi->nshi", back, qb, preferred_element_type=f32)
    grad_k = grad_k + jnp.einsum("nshj,nhij->nshi", vb, adjoint, preferred_element_type=f32)
    grad_v = jnp.einsum("nhts,nthj->nshj", scores, d_att, preferred_element_type=f32)
    grad_v = grad_v + jnp.einsum("nshi,nhij->nshj", kb, adjoint, preferred_element_type=f32)
    query_grad = grad_q.astype(jnp.bfloat16).reshape(rows, width)
    key_grad = grad_k.astype(jnp.bfloat16).reshape(rows, width)
    value_grad = grad_v.astype(jnp.bfloat16).reshape(rows, width)
    return (normed, query_grad, key_grad, value_grad)


def solution(mesh):
    return jax.shard_map(
        body,
        mesh=mesh,
        in_specs=(
            P("ctx", "head"),
            P("ctx", "head"),
            P("ctx", "head"),
            P("head"),
            P("ctx", "head"),
        ),
        out_specs=(P("ctx", "head"), P("ctx", "head"), P("ctx", "head"), P("ctx", "head")),
        check_vma=False,
    )
```

profile of v0, /device:TPU:1, one launch (start us, length us, event | category | flops | bytes accessed | tf_op | source)
XLA Modules:
  0.0 567.0 jit_solution(16652940304430302450)
XLA Ops:
  7.2 1.4 copy.100
  8.6 2.0 fusion.8
  11.9 1.3 copy-done.1
  13.2 1.8 convolution_bitcast_fusion.2
  15.0 195.0 %all-gather.5.cloned.1.call-done = f32[256,128,128]{2,1,0:T(8,128)} async-done(((f32[4,128,128]{2,1,0:T(8,128)}), f32[256,128,128]{2,1,0:T(8,128)}) %all-gather.5.cloned.1.call-update) | async-done | bytes 16777232 | tf_op jit(solution)/shard_map/all_gather | solution.py:12
  210.0 68.1 %while.30 = (s32[]{:T(128)}, f32[4,128,128]{2,1,0:T(8,128)S(1)}, s32[]{:T(128)}, f32[64,4,128,128]{3,2,1,0:T(8,128)}, s32[]{:T(128)}, /*index=5*/s32[]{:T(128)}) while((s32[]{:T(128)}, f32[4,128,128]{2,1,0:T(8,128)S(1)}, s32[]{:T(128)}, f32[64,4,128,128]{3,2,1,0:T(8,128)}, s32[]{:T(128)}, /*index=5*/s32[]{:T(128)}) %tuple.88), condition=%wide.region_1.2_spmd.clone, body=%wide.region_0.1_spmd.clone.sunk | while | flops 196612 | bytes 786533 | solution.py:21
  212.1 1.0 add_select_fusion.4
  214.2 1.0 add_select_fusion.4
  223.8 1.0 add_select_fusion.4
  226.0 1.0 add_select_fusion.4
  228.1 1.0 add_select_fusion.4
  230.2 1.0 add_select_fusion.4
  232.3 1.0 add_select_fusion.4
  234.5 1.0 add_select_fusion.4
  244.0 1.0 add_select_fusion.4
  246.2 1.0 add_select_fusion.4
  248.3 1.0 add_select_fusion.4
  250.4 1.0 add_select_fusion.4
  252.6 1.0 add_select_fusion.4
  254.7 1.0 add_select_fusion.4
  264.3 1.0 add_select_fusion.4
  266.4 1.0 add_select_fusion.4
  268.5 1.0 add_select_fusion.4
  270.7 1.0 add_select_fusion.4
  272.8 1.0 add_select_fusion.4
  274.9 1.0 add_select_fusion.4
  278.1 2.6 multiply_reduce_fusion
  280.7 12.8 %all-reduce = (f32[1,512]{1,0:T(1,128)S(1)}, f32[512]{0:T(512)S(1)}) all-reduce(f32[1,512]{1,0:T(1,128)S(1)} %bitcast.127, f32[512]{0:T(512)S(1)} %get-tuple-element.237), channel_id=1, replica_groups=mesh['ctx'=64,'head'=8] {'head'}, use_global_device_ids=true, to_apply=%region_3.4 | all-reduce | flops 1024 | bytes 8192 | tf_op jit(solution)/shard_map/psum | solution.py:53
  293.6 2.4 fusion.4
  299.9 2.3 fusion.1
  302.1 2.0 copy.50
  304.2 2.6 fusion.30
  307.3 178.7 %all-gather.7.cloned.1.call-done = f32[256,128,128]{2,1,0:T(8,128)} async-done(((f32[4,128,128]{2,1,0:T(8,128)}), f32[256,128,128]{2,1,0:T(8,128)}) %all-gather.7.cloned.1.call-update) | async-done | bytes 16777232 | tf_op jit(solution)/shard_map/all_gather | solution.py:12
  486.0 68.4 %while.31 = (s32[]{:T(128)}, f32[4,128,128]{2,1,0:T(8,128)S(1)}, s32[]{:T(128)}, f32[64,4,128,128]{3,2,1,0:T(8,128)}, s32[]{:T(128)}, /*index=5*/s32[]{:T(128)}, s32[]{:T(128)}, s32[]{:T(128)}) while((s32[]{:T(128)}, f32[4,128,128]{2,1,0:T(8,128)S(1)}, s32[]{:T(128)}, f32[64,4,128,128]{3,2,1,0:T(8,128)}, s32[]{:T(128)}, ...), condition=%wide.region_7.8_spmd.clone, body=%wide.region_6.7_spmd.clone.sunk | while | flops 196616 | bytes 786595 | solution.py:21
  488.1 1.0 add_select_fusion.5
  491.4 1.0 add_select_fusion.5
  494.6 1.0 add_select_fusion.5
  496.7 1.0 add_select_fusion.5
  499.9 1.0 add_select_fusion.5
  503.1 1.0 add_select_fusion.5
  508.5 1.0 add_select_fusion.5
  511.7 1.0 add_select_fusion.5
  514.9 1.0 add_select_fusion.5
  517.0 1.0 add_select_fusion.5
  520.2 1.0 add_select_fusion.5
  523.4 1.0 add_select_fusion.5
  554.4 2.4 fusion.3
  556.8 2.0 copy.52
  (144 shorter events, 106.8 us)
Async XLA Ops:
  7.2 3.9 copy-start
  7.2 3.9 copy-start.8
  7.2 3.6 copy-start.11
  7.2 202.8 %all-gather.5.cloned.1.call-start = ((), (), s32[]{:S(2)}) async-start(), calls=%async_computation | async-start | bytes 17039360 | tf_op jit(solution)/shard_map/all_gather | solution.py:12
  10.7 475.3 %all-gather.7.cloned.1.call-start = ((), (), s32[]{:S(2)}) async-start(), calls=%async_computation.1 | async-start | bytes 17039360 | tf_op jit(solution)/shard_map/all_gather | solution.py:12
  11.1 0.8 copy-start.12
  11.1 2.1 copy-start.6
  11.9 1.3 copy-start.1
  15.0 263.1 %copy-start.14 = (f32[512]{0:T(512)S(1)}, f32[512]{0:T(512)}, u32[]{:S(2)}) copy-start(f32[512]{0:T(512)} %param.12) | copy-start | bytes 6148
  295.9 3.1 copy-start.5
  295.9 1.2 copy-start.10
  295.9 2.2 copy-start.13
  299.0 3.1 copy-start.3
  299.9 4.3 copy-start.2
  304.2 2.6 copy-start.4
  307.3 247.1 %copy-start.9 = (bf16[512,512]{1,0:T(8,128)(2,1)S(1)}, bf16[512,512]{1,0:T(8,128)(2,1)}, u32[]{:S(2)}) copy-start(bf16[512,512]{1,0:T(8,128)(2,1)} %param.10) | copy-start | bytes 1572868
  554.4 4.5 copy-start.7
Sparse Core Ops, SparseCore 0:
  11.6 198.3 all-gather.4
  297.2 188.7 all-gather.6
where the time goes:
time: 571 us; the launch traced here: 567 us
  waiting for transfers between devices  374 us (65%)
  other arithmetic  136 us (24%)
  matrix products  17.2 us (3%)
  between operations  14.3 us (3%)
  blocking collectives  12.8 us (2%)
  local copies, waits for them, and re-layouts  9.98 us (2%)
    all_gather x2, waiting for transfers between devices, entering(): everything = lax.all_gather(value, axis)  374 us
    select_n x128, other arithmetic, turn(): return jnp.where(reached, new, before)  133 us
    psum x1, blocking collectives, body(): ssq, mdot = lax.psum((ssq_local, mdot_local), 'head')  12.8 us
  transfers between devices with their start and end apart: 2, of which 2 were waited for; matrix products, arithmetic and copies ran while one was open for 2% of the time, Pallas kernels for 0%

commit v1 on v0

v1 whole, which is shorter than its diff:
```python
import functools

import jax
import jax.numpy as jnp
from jax import lax
from jax.experimental import pallas as pl
from jax.experimental.pallas import tpu as pltpu
from jax.sharding import PartitionSpec as P

HD = 128
ROWS = 512
HEADS = 4
NY = 4
NZ = 16
NC = NY * NZ
NH = 8
FEATURES = 4096.0
MESH = pl.DeviceIdType.MESH
F32 = jnp.float32
BF16 = jnp.bfloat16


def dot(a, b, ca, cb):
    return lax.dot_general(a, b, (((ca,), (cb,)), ((), ())), preferred_element_type=F32)


def cols(h):
    return slice(h * HD, (h + 1) * HD)


def each_ctx_peer(y, z, visit):
    def turn(k, c):
        half = (k + 1) // 2
        dz = 8 + half * (1 - 2 * (k % 2))
        zz = (z + dz) % NZ
        for dy in (2, 1, 3, 0):
            visit(((y + dy) % NY) * NZ + zz)
        return c

    lax.fori_loop(0, NZ - 1, turn, 0)
    for dy in (2, 1, 3):
        visit(((y + dy) % NY) * NZ + z)


def each_head_peer(head, visit):
    for d in (4, 5, 3, 2, 6, 7, 1):
        visit((head + d) % NH)


def kernel(
    q_ref, k_ref, v_ref, gain_ref, g_ref,
    normed_ref, qg_ref, kg_ref, vg_ref,
    own, gathered, prefix, carry, scores, att, kgi, vgi, datt, norms, norms_in,
    send_sem, recv_sem, norm_send, norm_recv,
):
    ctx = lax.axis_index("ctx")
    head = lax.axis_index("head")
    y, z = ctx // NZ, ctx % NZ

    barrier = pltpu.get_barrier_semaphore()

    def greet(peer):
        pl.semaphore_signal(barrier, inc=1, device_id={"ctx": peer}, device_id_type=MESH)

    def greet_head(peer):
        pl.semaphore_signal(barrier, inc=1, device_id={"head": peer}, device_id_type=MESH)

    each_ctx_peer(y, z, greet)
    each_head_peer(head, greet_head)

    row = lax.broadcasted_iota(jnp.int32, (ROWS, ROWS), 0)
    col = lax.broadcasted_iota(jnp.int32, (ROWS, ROWS), 1)
    causal = row >= col

    def exchange(phase, src, dst, by_peer):
        def send(peer):
            pltpu.make_async_remote_copy(
                src_ref=src.at[phase // 2, peer],
                dst_ref=dst.at[phase // 2, ctx],
                send_sem=send_sem.at[phase],
                recv_sem=recv_sem.at[phase],
                device_id={"ctx": peer},
                device_id_type=MESH,
            ).start()

        each_ctx_peer(y, z, send)

    def arrived(phase, dst):
        view = dst.at[phase // 2, pl.ds(0, NC - 1)]
        pltpu.make_async_copy(view, view, recv_sem.at[phase]).wait()

    def sent(phase, src):
        view = src.at[phase // 2, pl.ds(0, NC - 1)]
        pltpu.make_async_copy(view, view, send_sem.at[phase]).wait()

    def scan(s, beside_out, beside_back):
        exchange(2 * s, own, gathered, True)
        gathered[s, ctx] = own[s, ctx]
        beside_out()
        arrived(2 * s, gathered)
        total = jnp.zeros((8, HD), F32)
        for t in range(NC) if s == 0 else range(NC - 1, -1, -1):
            prefix[s, t] = total
            total = total + gathered[s, t]
        exchange(2 * s + 1, prefix, carry, False)
        carry[s, ctx] = prefix[s, ctx]
        beside_back()
        arrived(2 * s + 1, carry)

    def state(s, h):
        return carry[s, 16 * h : 16 * (h + 1)].reshape(HD, HD).astype(BF16)

    for h in range(HEADS):
        kv = dot(k_ref[:, cols(h)], v_ref[:, cols(h)], 0, 0)
        own[0, 16 * h : 16 * (h + 1)] = kv.reshape(16, 8, HD)

    pl.semaphore_wait(barrier, NC - 1 + NH - 1)

    def forward_intra():
        for h in range(HEADS):
            c = cols(h)
            s = jnp.where(causal, dot(q_ref[:, c], k_ref[:, c], 1, 1), 0.0).astype(BF16)
            scores[h] = s
            att[:, c] = dot(s, v_ref[:, c], 1, 0)

    scan(0, forward_intra, lambda: None)

    ssq = jnp.zeros((ROWS, HD), F32)
    mdot = jnp.zeros((ROWS, HD), F32)
    for h in range(HEADS):
        c = cols(h)
        a = att[:, c] + dot(q_ref[:, c], state(0, h), 1, 0)
        att[:, c] = a
        u = g_ref[:, c].astype(F32) * gain_ref[:, c]
        ssq = ssq + a * a
        mdot = mdot + a * u
    ssq = jnp.sum(ssq, axis=1, keepdims=True)
    mdot = jnp.sum(mdot, axis=1, keepdims=True)
    lane = lax.broadcasted_iota(jnp.int32, (ROWS, HD), 1)
    both = jnp.where(lane < 4, ssq, mdot)
    mine = both.T[0:8]
    norms[...] = mine

    def send_norms(peer):
        pltpu.make_async_remote_copy(
            src_ref=norms,
            dst_ref=norms_in.at[head],
            send_sem=norm_send,
            recv_sem=norm_recv,
            device_id={"head": peer},
            device_id_type=MESH,
        ).start()

    each_head_peer(head, send_norms)
    norms_in[head] = mine
    seven = norms_in.at[pl.ds(0, NH - 1)]
    pltpu.make_async_copy(seven, seven, norm_recv).wait()
    total = norms_in[0]
    for t in range(1, NH):
        total = total + norms_in[t]
    rinv = lax.rsqrt(total[0:1] / FEATURES + 1e-6)
    slope = rinv * rinv * rinv * total[4:5] / FEATURES
    rinv = jnp.broadcast_to(rinv, (HD, ROWS)).T
    slope = jnp.broadcast_to(slope, (HD, ROWS)).T

    for h in range(HEADS):
        c = cols(h)
        u = g_ref[:, c].astype(F32) * gain_ref[:, c]
        d = (rinv * u - att[:, c] * slope).astype(BF16)
        datt[:, c] = d
        own[1, 16 * h : 16 * (h + 1)] = dot(q_ref[:, c], d, 0, 0).reshape(16, 8, HD)

    def backward_intra():
        for h in range(HEADS):
            c = cols(h)
            d = datt[:, c]
            normed_ref[:, c] = (att[:, c] * rinv * gain_ref[:, c]).astype(BF16)
            b = jnp.where(causal, dot(d, v_ref[:, c], 1, 1), 0.0).astype(BF16)
            qg_ref[:, c] = (dot(b, k_ref[:, c], 1, 0) + dot(d, state(0, h), 1, 1)).astype(BF16)
            kgi[:, c] = dot(b, q_ref[:, c], 0, 0)
            vgi[:, c] = dot(scores[h], d, 0, 0)

    scan(1, backward_intra, lambda: None)

    for h in range(HEADS):
        c = cols(h)
        adj = state(1, h)
        kg_ref[:, c] = (kgi[:, c] + dot(v_ref[:, c], adj, 1, 1)).astype(BF16)
        vg_ref[:, c] = (vgi[:, c] + dot(k_ref[:, c], adj, 1, 0)).astype(BF16)

    for s in (0, 1):
        sent(2 * s, own)
        sent(2 * s + 1, prefix)
    pltpu.make_async_copy(seven, seven, norm_send).wait()


def body(queries, keys, values, gain, out_grad):
    vmem = pl.BlockSpec(memory_space=pltpu.VMEM)
    out = jax.ShapeDtypeStruct((ROWS, HEADS * HD), BF16)
    wide = (ROWS, HEADS * HD)
    return pl.pallas_call(
        kernel,
        out_shape=(out,) * 4,
        in_specs=[vmem] * 5,
        out_specs=(vmem,) * 4,
        scratch_shapes=[
            pltpu.VMEM((2, NC, 8, HD), F32),
            pltpu.VMEM((2, NC, 8, HD), F32),
            pltpu.VMEM((2, NC, 8, HD), F32),
            pltpu.VMEM((2, NC, 8, HD), F32),
            pltpu.VMEM((HEADS, ROWS, ROWS), BF16),
            pltpu.VMEM(wide, F32),
            pltpu.VMEM(wide, F32),
            pltpu.VMEM(wide, F32),
            pltpu.VMEM(wide, BF16),
            pltpu.VMEM((8, ROWS), F32),
            pltpu.VMEM((NH, 8, ROWS), F32),
            pltpu.SemaphoreType.DMA((4,)),
            pltpu.SemaphoreType.DMA((4,)),
            pltpu.SemaphoreType.DMA,
            pltpu.SemaphoreType.DMA,
        ],
        compiler_params=pltpu.CompilerParams(
            collective_id=0, has_side_effects=True, vmem_limit_bytes=48 * 2**20
        ),
        name="linear_attention",
    )(queries, keys, values, gain.reshape(1, HEADS * HD), out_grad)


def solution(mesh):
    spec = P("ctx", "head")
    return jax.shard_map(
        body,
        mesh=mesh,
        in_specs=(spec, spec, spec, P("head"), spec),
        out_specs=(spec,) * 4,
        check_vma=False,
    )
```

time: 571 us -> 89.5 us (0.16)
  waiting for transfers between devices: 374 us -> 0 us
  other arithmetic: 136 us -> 0 us
  Pallas kernels: 0 us -> 80.5 us
  matrix products: 17.2 us -> 0 us
  between operations: 14.3 us -> 0.65 us
  blocking collectives: 12.8 us -> 0 us
    all_gather x2 -> x0, waiting for transfers between devices: 374 us -> none  [entering(): everything = lax.all_gather(value, axis)]
    select_n x128 -> x0, other arithmetic: 133 us -> none  [turn(): return jnp.where(reached, new, before)]
    pallas_call x0 -> x1, Pallas kernels: none -> 80.5 us  [body(): pl.pallas_call(kernel, out_shape=(out,) * 4, in_specs=[vmem] * 5, out_spe...]
    dot_general x12 -> x0, matrix products: 17.2 us -> none  [the longest x1 2.63 us: body(): jnp.einsum('nhts,nthj->nshj', scores, d_att, preferred_element_type=f32)]
    psum x1 -> x0, blocking collectives: 12.8 us -> none  [body(): ssq, mdot = lax.psum((ssq_local, mdot_local), 'head')]
  transfers between devices with their start and end apart: 2 -> 0, of which waited for: 2 -> 0; matrix products, arithmetic and copies ran while one was open for 2% -> 0% of each run, Pallas kernels for 0% -> 0%
where the time goes in v1:
time: 89.5 us; the launch traced here: 89.2 us
  Pallas kernels  80.5 us (90%)
  local copies, waits for them, and re-layouts  8.01 us (9%)
    pallas_call x1, Pallas kernels, body(): pl.pallas_call(kernel, out_shape=(out,) * 4, in_specs=[vmem] * 5, out_spe...  80.5 us
    unnamed x14, local copies, waits for them, and re-layouts  8.01 us

profile of v1, /device:TPU:1, one launch (start us, length us, event | category | flops | bytes accessed | tf_op | source)
XLA Modules:
  0.0 89.2 jit_solution(16592540095041774867)
XLA Ops:
  0.6 0.0 copy-start
  0.6 1.0 %copy-done = bf16[512,512]{1,0:T(8,128)(2,1)S(1)} copy-done((bf16[512,512]{1,0:T(8,128)(2,1)S(1)}, bf16[512,512]{1,0:T(8,128)(2,1)}, u32[]{:S(2)}) %copy-start) | copy-done | bytes 524312
  1.7 0.0 copy-start.1
  1.7 1.0 %copy-done.1 = bf16[512,512]{1,0:T(8,128)(2,1)S(1)} copy-done((bf16[512,512]{1,0:T(8,128)(2,1)S(1)}, bf16[512,512]{1,0:T(8,128)(2,1)}, u32[]{:S(2)}) %copy-start.1) | copy-done | bytes 524312
  2.7 0.0 copy-start.2
  2.7 1.0 %copy-done.2 = bf16[512,512]{1,0:T(8,128)(2,1)S(1)} copy-done((bf16[512,512]{1,0:T(8,128)(2,1)S(1)}, bf16[512,512]{1,0:T(8,128)(2,1)}, u32[]{:S(2)}) %copy-start.2) | copy-done | bytes 524312
  3.8 0.0 copy-start.3
  3.8 1.0 %copy-done.3 = bf16[512,512]{1,0:T(8,128)(2,1)S(1)} copy-done((bf16[512,512]{1,0:T(8,128)(2,1)S(1)}, bf16[512,512]{1,0:T(8,128)(2,1)}, u32[]{:S(2)}) %copy-start.3) | copy-done | bytes 524312
  4.8 0.0 copy-start.4
  4.8 0.7 copy-done.4
  5.5 80.5 %linear_attention.1 = (bf16[512,512]{1,0:T(8,128)(2,1)S(1)}, bf16[512,512]{1,0:T(8,128)(2,1)S(1)}, bf16[512,512]{1,0:T(8,128)(2,1)S(1)}, bf16[512,512]{1,0:T(8,128)(2,1)S(1)}) custom-call(bf16[512,512]{1,0:T(8,128)(2,1)S(1)} %copy-done, bf16[512,512]{1,0:T(8,128)(2,1)S(1)} %copy-done.1, bf16[512,512]{1,0:T(8,128)(2,1)S(1)} %copy-done.2, ...), custom_call_target="tpu_custom_call" | custom-call | tf_op jit(solution)/shard_map/linear_attention/pallas_call | solution.py:201
  86.0 0.8 copy.13
  86.8 0.8 copy.14
  87.6 0.8 copy.15
  88.4 0.8 copy.16
Async XLA Ops:
  0.6 1.0 %copy-start = (bf16[512,512]{1,0:T(8,128)(2,1)S(1)}, bf16[512,512]{1,0:T(8,128)(2,1)}, u32[]{:S(2)}) copy-start(bf16[512,512]{1,0:T(8,128)(2,1)} %q_ref.1) | copy-start | bytes 1572868
  1.7 1.0 %copy-start.1 = (bf16[512,512]{1,0:T(8,128)(2,1)S(1)}, bf16[512,512]{1,0:T(8,128)(2,1)}, u32[]{:S(2)}) copy-start(bf16[512,512]{1,0:T(8,128)(2,1)} %k_ref.1) | copy-start | bytes 1572868
  2.7 1.0 %copy-start.2 = (bf16[512,512]{1,0:T(8,128)(2,1)S(1)}, bf16[512,512]{1,0:T(8,128)(2,1)}, u32[]{:S(2)}) copy-start(bf16[512,512]{1,0:T(8,128)(2,1)} %v_ref.1) | copy-start | bytes 1572868
  3.8 1.0 %copy-start.3 = (bf16[512,512]{1,0:T(8,128)(2,1)S(1)}, bf16[512,512]{1,0:T(8,128)(2,1)}, u32[]{:S(2)}) copy-start(bf16[512,512]{1,0:T(8,128)(2,1)} %g_ref.1) | copy-start | bytes 1572868
  4.8 0.7 copy-start.4

commit v2 on v1

v2 whole, which is shorter than its diff:
```python
import functools

import jax
import jax.numpy as jnp
from jax import lax
from jax.experimental import pallas as pl
from jax.experimental.pallas import tpu as pltpu
from jax.sharding import PartitionSpec as P

HD = 128
ROWS = 512
HEADS = 4
NY = 4
NZ = 16
REACH = 4
WINDOW = 2 * REACH
TILES = NY * WINDOW
TILE = HD // TILES
NEIGHBOURS = TILES - 1 + NY + 1
NH = 8
FEATURES = 4096.0
PIECES = 2
MESH = pl.DeviceIdType.MESH
F32 = jnp.float32
BF16 = jnp.bfloat16


def dot(a, b, ca, cb):
    return lax.dot_general(a, b, (((ca,), (cb,)), ((), ())), preferred_element_type=F32)


def cols(h):
    return slice(h * HD, (h + 1) * HD)


def each_in_window(y, z, sign, visit):
    def turn(k, c):
        dz = jnp.where(k % 2 == 0, REACH - k // 2, k // 2 - (REACH - 1)) * sign
        for dy in (2, 1, 3, 0):
            visit((y + dy) % NY, (z + dz + NZ) % NZ)
        return c

    lax.fori_loop(0, 2 * REACH - 1, turn, 0)
    for dy in (2, 1, 3):
        visit((y + dy) % NY, z)


def each_neighbour(y, z, visit):
    each_in_window(y, z, 1, visit)
    for dy in (2, 1, 3, 0):
        visit((y + dy) % NY, (z + NZ - REACH) % NZ)
    visit(y, (z + NZ // 2) % NZ)


def tile_of(y, z):
    return y * WINDOW + z % WINDOW


def each_head_peer(head, visit):
    for d in (4, 5, 3, 2, 6, 7, 1):
        visit((head + d) % NH)


def kernel(
    q_hbm, k_hbm, v_hbm, gain_hbm, g_hbm,
    normed_hbm, qg_hbm, kg_hbm, vg_hbm,
    q_ref, k_ref, v_ref, gain_ref, g_ref, normed_ref, qg_ref, kg_ref, vg_ref,
    own, gathered, rows_out, rows_in, sums, carry, scores, att, kgi, vgi, datt, norms, norms_in,
    load_sem, store_sem, out_send, out_recv, row_send, row_recv, back_send, back_recv,
    norm_send, norm_recv,
):
    ctx = lax.axis_index("ctx")
    head = lax.axis_index("head")
    y, z = ctx // NZ, ctx % NZ
    mine = tile_of(y, z)

    loads = [
        pltpu.make_async_copy(src, dst, load_sem.at[i])
        for i, (src, dst) in enumerate(
            ((k_hbm, k_ref), (v_hbm, v_ref), (q_hbm, q_ref), (g_hbm, g_ref), (gain_hbm, gain_ref))
        )
    ]
    for load in loads:
        load.start()

    barrier = pltpu.get_barrier_semaphore()

    def greet(py, pz):
        pl.semaphore_signal(
            barrier, inc=1, device_id={"ctx": py * NZ + pz}, device_id_type=MESH
        )

    def greet_head(peer):
        pl.semaphore_signal(barrier, inc=1, device_id={"head": peer}, device_id_type=MESH)

    each_neighbour(y, z, greet)
    each_head_peer(head, greet_head)

    row = lax.broadcasted_iota(jnp.int32, (ROWS, ROWS), 0)
    col = lax.broadcasted_iota(jnp.int32, (ROWS, ROWS), 1)
    causal = row >= col

    member = [(z + j + NZ - REACH) % NZ for j in range(WINDOW)]
    wraps = jnp.logical_or(z < REACH, z > NZ - REACH)
    other = (z + NZ // 2) % NZ
    other_wraps = jnp.logical_or(other < REACH, other > NZ - REACH)

    def send_out(s, h):
        def send(py, pz):
            pltpu.make_async_remote_copy(
                src_ref=own.at[s, h, tile_of(py, pz)],
                dst_ref=gathered.at[s, h, y * WINDOW + (z - pz + REACH + NZ) % NZ],
                send_sem=out_send.at[s, h],
                recv_sem=out_recv.at[s, h],
                device_id={"ctx": py * NZ + pz},
                device_id_type=MESH,
            ).start()

        each_in_window(y, z, 1, send)

    def row_copy(s, h):
        return pltpu.make_async_remote_copy(
            src_ref=rows_out.at[s, h],
            dst_ref=rows_in.at[s, h],
            send_sem=row_send.at[s, h],
            recv_sem=row_recv.at[s, h],
            device_id={"ctx": y * NZ + other},
            device_id_type=MESH,
        )

    def add_window(s, h):
        gathered[s, h, y * WINDOW + REACH] = own[s, h, mine]
        view = gathered.at[s, h, pl.ds(0, TILES - 1)]
        pltpu.make_async_copy(view, view, out_recv.at[s, h]).wait()
        zero = jnp.zeros((TILE, HD), F32)
        order = range(WINDOW) if s == 0 else range(WINDOW - 1, -1, -1)
        before = zero
        for r in range(NY):
            at = (r if s == 0 else NY - 1 - r) * WINDOW
            first, whole = zero, zero
            for j in order:
                value = gathered[s, h, at + j]
                leads = member[j] < REACH * 2 if s == 0 else member[j] >= REACH * 2
                first = first + jnp.where(leads, value, 0.0)
                whole = whole + value
            rows_out[s, h, r] = before + jnp.where(wraps, first, whole)
            running = zero
            for j in order:
                leads = member[j] < REACH * 2 if s == 0 else member[j] >= REACH * 2
                start = member[j] == (0 if s == 0 else NZ - 1)
                running = jnp.where(start, 0.0, running)
                extra = jnp.where(jnp.logical_and(wraps, jnp.logical_not(leads)), first, 0.0)
                sums[s, h, at + j] = before + extra + running
                running = running + gathered[s, h, at + j]
            before = before + whole
        row_copy(s, h).start()

    def send_back(s, h):
        view = rows_in.at[s, h]
        pltpu.make_async_copy(view, view, row_recv.at[s, h]).wait()
        for j in range(WINDOW):
            passed = other < member[j] if s == 0 else other > member[j]
            passed = jnp.logical_or(passed, other_wraps)
            for r in range(NY):
                at = (r if s == 0 else NY - 1 - r) * WINDOW + j
                prior = rows_in[s, h, r - 1] if r else jnp.zeros((TILE, HD), F32)
                sums[s, h, at] = sums[s, h, at] + jnp.where(passed, rows_in[s, h, r], prior)

        def send(py, pz):
            pltpu.make_async_remote_copy(
                src_ref=sums.at[s, h, py * WINDOW + (pz - z + REACH + NZ) % NZ],
                dst_ref=carry.at[s, h, mine],
                send_sem=back_send.at[s, h],
                recv_sem=back_recv.at[s, h],
                device_id={"ctx": py * NZ + pz},
                device_id_type=MESH,
            ).start()

        each_in_window(y, z, -1, send)
        pltpu.make_async_copy(
            sums.at[s, h, y * WINDOW + REACH], carry.at[s, h, mine], back_recv.at[s, h]
        ).start()

    def arrived(s, h):
        view = carry.at[s, h]
        pltpu.make_async_copy(view, view, back_recv.at[s, h]).wait()

    def add_up(s):
        for h in range(HEADS):
            add_window(s, h)
        for h in range(HEADS):
            send_back(s, h)

    def state(s, h):
        return carry[s, h].reshape(HD, HD).astype(BF16)

    def store(i, src, dst, c):
        return pltpu.make_async_copy(src.at[:, c], dst.at[:, c], store_sem.at[i])

    loads[0].wait()
    loads[1].wait()
    for h in range(HEADS):
        kv = dot(k_ref[:, cols(h)], v_ref[:, cols(h)], 0, 0)
        own[0, h] = kv.reshape(TILES, TILE, HD)
        if h == 0:
            pl.semaphore_wait(barrier, NEIGHBOURS + NH - 1)
        send_out(0, h)

    for load in loads[2:]:
        load.wait()
    for h in range(HEADS):
        c = cols(h)
        s = jnp.where(causal, dot(q_ref[:, c], k_ref[:, c], 1, 1), 0.0).astype(BF16)
        scores[h] = s
        att[:, c] = dot(s, v_ref[:, c], 1, 0)

    add_up(0)

    ssq = jnp.zeros((ROWS, HD), F32)
    mdot = jnp.zeros((ROWS, HD), F32)
    for h in range(HEADS):
        arrived(0, h)
        c = cols(h)
        a = att[:, c] + dot(q_ref[:, c], state(0, h), 1, 0)
        att[:, c] = a
        u = g_ref[:, c].astype(F32) * gain_ref[:, c]
        ssq = ssq + a * a
        mdot = mdot + a * u
    ssq = jnp.sum(ssq, axis=1, keepdims=True)
    mdot = jnp.sum(mdot, axis=1, keepdims=True)
    lane = lax.broadcasted_iota(jnp.int32, (ROWS, HD), 1)
    flat = jnp.where(lane < 4, ssq, mdot).T[0:8]
    line = lax.broadcasted_iota(jnp.int32, (8, HD), 0) % 4
    packed = flat[:, 0:HD]
    for b in range(1, 4):
        packed = jnp.where(line == b, flat[:, b * HD : (b + 1) * HD], packed)
    norms[...] = packed

    def send_norms(peer):
        pltpu.make_async_remote_copy(
            src_ref=norms,
            dst_ref=norms_in.at[head],
            send_sem=norm_send,
            recv_sem=norm_recv,
            device_id={"head": peer},
            device_id_type=MESH,
        ).start()

    each_head_peer(head, send_norms)
    norms_in[head] = packed
    seven = norms_in.at[pl.ds(0, NH - 1)]
    pltpu.make_async_copy(seven, seven, norm_recv).wait()
    total = norms_in[0]
    for t in range(1, NH):
        total = total + norms_in[t]
    inv = lax.rsqrt(total[0:4] / FEATURES + 1e-6)
    slp = inv * inv * inv * total[4:8] / FEATURES

    def column(x):
        return jnp.concatenate(
            [jnp.broadcast_to(x[b : b + 1], (HD, HD)).T for b in range(4)], axis=0
        )

    rinv = column(inv)
    slope = column(slp)

    for h in range(HEADS):
        c = cols(h)
        u = g_ref[:, c].astype(F32) * gain_ref[:, c]
        d = (rinv * u - att[:, c] * slope).astype(BF16)
        datt[:, c] = d
        own[1, h] = dot(q_ref[:, c], d, 0, 0).reshape(TILES, TILE, HD)
        send_out(1, h)

    for h in range(HEADS):
        c = cols(h)
        d = datt[:, c]
        normed_ref[:, c] = (att[:, c] * rinv * gain_ref[:, c]).astype(BF16)
        b = jnp.where(causal, dot(d, v_ref[:, c], 1, 1), 0.0).astype(BF16)
        qg_ref[:, c] = (dot(b, k_ref[:, c], 1, 0) + dot(d, state(0, h), 1, 1)).astype(BF16)
        kgi[:, c] = dot(b, q_ref[:, c], 0, 0)
        vgi[:, c] = dot(scores[h], d, 0, 0)

    stores = [
        store(i, src, dst, slice(None))
        for i, (src, dst) in enumerate(((normed_ref, normed_hbm), (qg_ref, qg_hbm)))
    ]
    for copy in stores:
        copy.start()

    add_up(1)

    for h in range(HEADS):
        arrived(1, h)
        c = cols(h)
        adj = state(1, h)
        kg_ref[:, c] = (kgi[:, c] + dot(v_ref[:, c], adj, 1, 1)).astype(BF16)
        vg_ref[:, c] = (vgi[:, c] + dot(k_ref[:, c], adj, 1, 0)).astype(BF16)
        for i, (src, dst) in enumerate(((kg_ref, kg_hbm), (vg_ref, vg_hbm))):
            stores.append(store(2 + 2 * h + i, src, dst, c))
            stores[-1].start()

    for s in range(2):
        for h in range(HEADS):
            view = own.at[s, h, pl.ds(0, TILES - 1)]
            pltpu.make_async_copy(view, view, out_send.at[s, h]).wait()
            pltpu.make_async_copy(view, view, back_send.at[s, h]).wait()
            row_copy(s, h).wait_send()
    pltpu.make_async_copy(seven, seven, norm_send).wait()
    for copy in stores:
        copy.wait()


def write_out(a, b, c, d, a_out, b_out, c_out, d_out, held, in_sem, out_sem):
    step = ROWS // PIECES
    loads, stores = [], []
    for i, (src, dst) in enumerate(((a, a_out), (b, b_out), (c, c_out), (d, d_out))):
        for j in range(PIECES):
            rows = pl.ds(j * step, step)
            at = PIECES * i + j
            loads.append(pltpu.make_async_copy(src.at[rows], held.at[i, rows], in_sem.at[at]))
            stores.append(pltpu.make_async_copy(held.at[i, rows], dst.at[rows], out_sem.at[at]))
    for load in loads:
        load.start()
    for load, store in zip(loads, stores):
        load.wait()
        store.start()
    for store in stores:
        store.wait()


def body(queries, keys, values, gain, out_grad):
    hbm = pl.BlockSpec(memory_space=pltpu.HBM)
    out = jax.ShapeDtypeStruct((ROWS, HEADS * HD), BF16)
    wide = (ROWS, HEADS * HD)
    results = pl.pallas_call(
        kernel,
        out_shape=(out,) * 4,
        in_specs=[hbm] * 5,
        out_specs=(hbm,) * 4,
        scratch_shapes=[
            pltpu.VMEM(wide, BF16),
            pltpu.VMEM(wide, BF16),
            pltpu.VMEM(wide, BF16),
            pltpu.VMEM((1, HEADS * HD), F32),
            pltpu.VMEM(wide, BF16),
            pltpu.VMEM(wide, BF16),
            pltpu.VMEM(wide, BF16),
            pltpu.VMEM(wide, BF16),
            pltpu.VMEM(wide, BF16),
            pltpu.VMEM((2, HEADS, TILES, TILE, HD), F32),
            pltpu.VMEM((2, HEADS, TILES, TILE, HD), F32),
            pltpu.VMEM((2, HEADS, NY, TILE, HD), F32),
            pltpu.VMEM((2, HEADS, NY, TILE, HD), F32),
            pltpu.VMEM((2, HEADS, TILES, TILE, HD), F32),
            pltpu.VMEM((2, HEADS, TILES, TILE, HD), F32),
            pltpu.VMEM((HEADS, ROWS, ROWS), BF16),
            pltpu.VMEM(wide, F32),
            pltpu.VMEM(wide, F32),
            pltpu.VMEM(wide, F32),
            pltpu.VMEM(wide, BF16),
            pltpu.VMEM((8, HD), F32),
            pltpu.VMEM((NH, 8, HD), F32),
            pltpu.SemaphoreType.DMA((5,)),
            pltpu.SemaphoreType.DMA((2 + 2 * HEADS,)),
        ]
        + [pltpu.SemaphoreType.DMA((2, HEADS))] * 6
        + [
            pltpu.SemaphoreType.DMA,
            pltpu.SemaphoreType.DMA,
        ],
        compiler_params=pltpu.CompilerParams(
            collective_id=0, has_side_effects=True, vmem_limit_bytes=62 * 2**20
        ),
        name="linear_attention",
    )(queries, keys, values, gain.reshape(1, HEADS * HD), out_grad)
    return pl.pallas_call(
        write_out,
        out_shape=(out,) * 4,
        in_specs=[hbm] * 4,
        out_specs=(hbm,) * 4,
        scratch_shapes=[
            pltpu.VMEM((4,) + wide, BF16),
            pltpu.SemaphoreType.DMA((4 * PIECES,)),
            pltpu.SemaphoreType.DMA((4 * PIECES,)),
        ],
        name="write_out",
    )(*results)


def solution(mesh):
    spec = P("ctx", "head")
    return jax.shard_map(
        body,
        mesh=mesh,
        in_specs=(spec, spec, spec, P("head"), spec),
        out_specs=(spec,) * 4,
        check_vma=False,
    )
```

time: 89.5 us -> 74.4 us (0.83)
  the two profiles are of different devices: /device:TPU:1 before, /device:TPU:32 now
where the time goes in v2:
time: 74.4 us; the launch traced here: 74.3 us
  Pallas kernels  73.6 us (99%)
    pallas_call x1, Pallas kernels, body(): pl.pallas_call(kernel, out_shape=(out,) * 4, in_specs=[hbm] * 5, out_spec...  71.2 us
    pallas_call x1, Pallas kernels, body(): pl.pallas_call(write_out, out_shape=(out,) * 4, in_specs=[hbm] * 4, out_s...  2.4 us

profile of v2, /device:TPU:32, one launch (start us, length us, event | category | flops | bytes accessed | tf_op | source)
XLA Modules:
  0.0 74.3 jit_solution(10238344929810642038)
XLA Ops:
  0.6 71.2 %linear_attention.1 = (bf16[512,512]{1,0:T(8,128)(2,1)}, bf16[512,512]{1,0:T(8,128)(2,1)}, bf16[512,512]{1,0:T(8,128)(2,1)}, bf16[512,512]{1,0:T(8,128)(2,1)}) custom-call(bf16[512,512]{1,0:T(8,128)(2,1)} %q_hbm.1, bf16[512,512]{1,0:T(8,128)(2,1)} %k_hbm.1, bf16[512,512]{1,0:T(8,128)(2,1)} %v_hbm.1, f32[1,512]{1,0:T(1,128)} %bitcast.1, bf16[512,512]{1,0:T(8,128)(2,1)} %g_hbm.1), custom_call_target="tpu_custom_call" | custom-call | tf_op jit(solution)/shard_map/linear_attention/pallas_call | solution.py:336
  71.9 2.4 %write_out.1 = (bf16[512,512]{1,0:T(8,128)(2,1)}, bf16[512,512]{1,0:T(8,128)(2,1)}, bf16[512,512]{1,0:T(8,128)(2,1)}, bf16[512,512]{1,0:T(8,128)(2,1)}) custom-call(bf16[512,512]{1,0:T(8,128)(2,1)} %get-tuple-element.8.a, bf16[512,512]{1,0:T(8,128)(2,1)} %get-tuple-element.9.b, bf16[512,512]{1,0:T(8,128)(2,1)} %get-tuple-element.10.c, ...), custom_call_target="tpu_custom_call" | custom-call | tf_op jit(solution)/shard_map/write_out/pallas_call | solution.py:377

commit v3 on v2

--- a/solution.py
+++ b/solution.py
@@ -33,32 +33,45 @@
     return slice(h * HD, (h + 1) * HD)
 
 
+def wrap(i, n):
+    return lax.rem(i, n)
+
+
 def each_in_window(y, z, sign, visit):
     def turn(k, c):
-        dz = jnp.where(k % 2 == 0, REACH - k // 2, k // 2 - (REACH - 1)) * sign
+        half, odd = lax.div(k, 2), lax.rem(k, 2)
+        dz = (REACH - half + odd * (2 * half - 2 * REACH + 1)) * sign
         for dy in (2, 1, 3, 0):
-            visit((y + dy) % NY, (z + dz + NZ) % NZ)
+            visit(wrap(y + dy, NY), wrap(z + dz + NZ, NZ))
         return c
 
     lax.fori_loop(0, 2 * REACH - 1, turn, 0)
     for dy in (2, 1, 3):
-        visit((y + dy) % NY, z)
+        visit(wrap(y + dy, NY), z)
+
+
+def side(z):
+    return 1 - 2 * lax.rem(z, 2)
+
+
+def below(z):
+    return REACH - lax.rem(z, 2)
 
 
 def each_neighbour(y, z, visit):
     each_in_window(y, z, 1, visit)
     for dy in (2, 1, 3, 0):
-        visit((y + dy) % NY, (z + NZ - REACH) % NZ)
-    visit(y, (z + NZ // 2) % NZ)
+        visit(wrap(y + dy, NY), wrap(z + NZ - REACH, NZ))
+    visit(y, wrap(z + NZ // 2, NZ))
 
 
 def tile_of(y, z):
-    return y * WINDOW + z % WINDOW
+    return y * WINDOW + wrap(z, WINDOW)
 
 
 def each_head_peer(head, visit):
     for d in (4, 5, 3, 2, 6, 7, 1):
-        visit((head + d) % NH)
+        visit(wrap(head + d, NH))
 
 
 def kernel(
@@ -71,7 +84,7 @@
 ):
     ctx = lax.axis_index("ctx")
     head = lax.axis_index("head")
-    y, z = ctx // NZ, ctx % NZ
+    y, z = lax.div(ctx, NZ), lax.rem(ctx, NZ)
     mine = tile_of(y, z)
 
     loads = [
@@ -100,23 +113,24 @@
     col = lax.broadcasted_iota(jnp.int32, (ROWS, ROWS), 1)
     causal = row >= col
 
-    member = [(z + j + NZ - REACH) % NZ for j in range(WINDOW)]
-    wraps = jnp.logical_or(z < REACH, z > NZ - REACH)
-    other = (z + NZ // 2) % NZ
-    other_wraps = jnp.logical_or(other < REACH, other > NZ - REACH)
+    low = below(z)
+    member = [wrap(z + j + NZ - low, NZ) for j in range(WINDOW)]
+    wraps = jnp.logical_or(z < low, z > WINDOW + low)
+    other = wrap(z + NZ // 2, NZ)
+    other_wraps = jnp.logical_or(other < low, other > WINDOW + low)
 
     def send_out(s, h):
         def send(py, pz):
             pltpu.make_async_remote_copy(
                 src_ref=own.at[s, h, tile_of(py, pz)],
-                dst_ref=gathered.at[s, h, y * WINDOW + (z - pz + REACH + NZ) % NZ],
+                dst_ref=gathered.at[s, h, y * WINDOW + wrap(z - pz + below(pz) + NZ, NZ)],
                 send_sem=out_send.at[s, h],
                 recv_sem=out_recv.at[s, h],
                 device_id={"ctx": py * NZ + pz},
                 device_id_type=MESH,
             ).start()
 
-        each_in_window(y, z, 1, send)
+        each_in_window(y, z, side(z), send)
 
     def row_copy(s, h):
         return pltpu.make_async_remote_copy(
@@ -129,7 +143,7 @@
         )
 
     def add_window(s, h):
-        gathered[s, h, y * WINDOW + REACH] = own[s, h, mine]
+        gathered[s, h, y * WINDOW + low] = own[s, h, mine]
         view = gathered.at[s, h, pl.ds(0, TILES - 1)]
         pltpu.make_async_copy(view, view, out_recv.at[s, h]).wait()
         zero = jnp.zeros((TILE, HD), F32)
@@ -168,7 +182,7 @@
 
         def send(py, pz):
             pltpu.make_async_remote_copy(
-                src_ref=sums.at[s, h, py * WINDOW + (pz - z + REACH + NZ) % NZ],
+                src_ref=sums.at[s, h, py * WINDOW + wrap(pz - z + low + NZ, NZ)],
                 dst_ref=carry.at[s, h, mine],
                 send_sem=back_send.at[s, h],
                 recv_sem=back_recv.at[s, h],
@@ -176,9 +190,9 @@
                 device_id_type=MESH,
             ).start()
 
-        each_in_window(y, z, -1, send)
+        each_in_window(y, z, -side(z), send)
         pltpu.make_async_copy(
-            sums.at[s, h, y * WINDOW + REACH], carry.at[s, h, mine], back_recv.at[s, h]
+            sums.at[s, h, y * WINDOW + low], carry.at[s, h, mine], back_recv.at[s, h]
         ).start()
 
     def arrived(s, h):

time: 74.4 us -> 71.2 us (0.957)
  the two profiles are of different devices: /device:TPU:32 before, /device:TPU:1 now
where the time goes in v3:
time: 71.2 us; the launch traced here: 70.6 us
  Pallas kernels  70 us (98%)
    pallas_call x1, Pallas kernels, body(): pl.pallas_call(kernel, out_shape=(out,) * 4, in_specs=[hbm] * 5, out_spec...  67.6 us
    pallas_call x1, Pallas kernels, body(): pl.pallas_call(write_out, out_shape=(out,) * 4, in_specs=[hbm] * 4, out_s...  2.4 us

profile of v3, /device:TPU:1, one launch (start us, length us, event | category | flops | bytes accessed | tf_op | source)
XLA Modules:
  0.0 70.6 jit_solution(4033713255155016355)
XLA Ops:
  0.6 67.6 %linear_attention.1 = (bf16[512,512]{1,0:T(8,128)(2,1)}, bf16[512,512]{1,0:T(8,128)(2,1)}, bf16[512,512]{1,0:T(8,128)(2,1)}, bf16[512,512]{1,0:T(8,128)(2,1)}) custom-call(bf16[512,512]{1,0:T(8,128)(2,1)} %q_hbm.1, bf16[512,512]{1,0:T(8,128)(2,1)} %k_hbm.1, bf16[512,512]{1,0:T(8,128)(2,1)} %v_hbm.1, f32[1,512]{1,0:T(1,128)} %bitcast.1, bf16[512,512]{1,0:T(8,128)(2,1)} %g_hbm.1), custom_call_target="tpu_custom_call" | custom-call | tf_op jit(solution)/shard_map/linear_attention/pallas_call | solution.py:350
  68.2 2.4 %write_out.1 = (bf16[512,512]{1,0:T(8,128)(2,1)}, bf16[512,512]{1,0:T(8,128)(2,1)}, bf16[512,512]{1,0:T(8,128)(2,1)}, bf16[512,512]{1,0:T(8,128)(2,1)}) custom-call(bf16[512,512]{1,0:T(8,128)(2,1)} %get-tuple-element.8.a, bf16[512,512]{1,0:T(8,128)(2,1)} %get-tuple-element.9.b, bf16[512,512]{1,0:T(8,128)(2,1)} %get-tuple-element.10.c, ...), custom_call_target="tpu_custom_call" | custom-call | tf_op jit(solution)/shard_map/write_out/pallas_call | solution.py:391

commit v4 on v3

--- a/solution.py
+++ b/solution.py
@@ -16,7 +16,7 @@
 WINDOW = 2 * REACH
 TILES = NY * WINDOW
 TILE = HD // TILES
-NEIGHBOURS = TILES - 1 + NY + 1
+NEIGHBOURS = TILES - 1 + NY
 NH = 8
 FEATURES = 4096.0
 PIECES = 2
@@ -62,7 +62,6 @@
     each_in_window(y, z, 1, visit)
     for dy in (2, 1, 3, 0):
         visit(wrap(y + dy, NY), wrap(z + NZ - REACH, NZ))
-    visit(y, wrap(z + NZ // 2, NZ))
 
 
 def tile_of(y, z):
@@ -86,6 +85,8 @@
     head = lax.axis_index("head")
     y, z = lax.div(ctx, NZ), lax.rem(ctx, NZ)
     mine = tile_of(y, z)
+    core = lax.rem(head, 2)
+    home_head = head + 1 - core
 
     loads = [
         pltpu.make_async_copy(src, dst, load_sem.at[i])
@@ -98,15 +99,20 @@
 
     barrier = pltpu.get_barrier_semaphore()
 
+    def greet_at(py, pz, to):
+        pl.semaphore_signal(
+            barrier, inc=1, device_id={"ctx": py * NZ + pz, "head": to}, device_id_type=MESH
+        )
+
     def greet(py, pz):
-        pl.semaphore_signal(
-            barrier, inc=1, device_id={"ctx": py * NZ + pz}, device_id_type=MESH
-        )
+        greet_at(py, pz, home_head)
+        pl.when(core == 1)(lambda: greet_at(py, pz, head - 1))
 
     def greet_head(peer):
         pl.semaphore_signal(barrier, inc=1, device_id={"head": peer}, device_id_type=MESH)
 
     each_neighbour(y, z, greet)
+    pl.when(core == 1)(lambda: greet_at(y, wrap(z + NZ // 2, NZ), head))
     each_head_peer(head, greet_head)
 
     row = lax.broadcasted_iota(jnp.int32, (ROWS, ROWS), 0)
@@ -123,29 +129,31 @@
         def send(py, pz):
             pltpu.make_async_remote_copy(
                 src_ref=own.at[s, h, tile_of(py, pz)],
-                dst_ref=gathered.at[s, h, y * WINDOW + wrap(z - pz + below(pz) + NZ, NZ)],
+                dst_ref=gathered.at[s, core, h, y * WINDOW + wrap(z - pz + below(pz) + NZ, NZ)],
                 send_sem=out_send.at[s, h],
-                recv_sem=out_recv.at[s, h],
-                device_id={"ctx": py * NZ + pz},
+                recv_sem=out_recv.at[s, core, h],
+                device_id={"ctx": py * NZ + pz, "head": home_head},
                 device_id_type=MESH,
             ).start()
 
         each_in_window(y, z, side(z), send)
-
-    def row_copy(s, h):
+        pl.when(core == 0)(lambda: send(y, z))
+
+    def row_copy(s, c, h):
         return pltpu.make_async_remote_copy(
-            src_ref=rows_out.at[s, h],
-            dst_ref=rows_in.at[s, h],
-            send_sem=row_send.at[s, h],
-            recv_sem=row_recv.at[s, h],
+            src_ref=rows_out.at[s, c, h],
+            dst_ref=rows_in.at[s, c, h],
+            send_sem=row_send.at[s, c, h],
+            recv_sem=row_recv.at[s, c, h],
             device_id={"ctx": y * NZ + other},
             device_id_type=MESH,
         )
 
-    def add_window(s, h):
-        gathered[s, h, y * WINDOW + low] = own[s, h, mine]
-        view = gathered.at[s, h, pl.ds(0, TILES - 1)]
-        pltpu.make_async_copy(view, view, out_recv.at[s, h]).wait()
+    def add_window(s, c, h):
+        if c == 1:
+            gathered[s, c, h, y * WINDOW + low] = own[s, h, mine]
+        view = gathered.at[s, c, h, pl.ds(0, TILES - c)]
+        pltpu.make_async_copy(view, view, out_recv.at[s, c, h]).wait()
         zero = jnp.zeros((TILE, HD), F32)
         order = range(WINDOW) if s == 0 else range(WINDOW - 1, -1, -1)
         before = zero
@@ -153,57 +161,64 @@
             at = (r if s == 0 else NY - 1 - r) * WINDOW
             first, whole = zero, zero
             for j in order:
-                value = gathered[s, h, at + j]
+                value = gathered[s, c, h, at + j]
                 leads = member[j] < REACH * 2 if s == 0 else member[j] >= REACH * 2
                 first = first + jnp.where(leads, value, 0.0)
                 whole = whole + value
-            rows_out[s, h, r] = before + jnp.where(wraps, first, whole)
+            rows_out[s, c, h, r] = before + jnp.where(wraps, first, whole)
             running = zero
             for j in order:
                 leads = member[j] < REACH * 2 if s == 0 else member[j] >= REACH * 2
                 start = member[j] == (0 if s == 0 else NZ - 1)
                 running = jnp.where(start, 0.0, running)
                 extra = jnp.where(jnp.logical_and(wraps, jnp.logical_not(leads)), first, 0.0)
-                sums[s, h, at + j] = before + extra + running
-                running = running + gathered[s, h, at + j]
+                sums[s, c, h, at + j] = before + extra + running
+                running = running + gathered[s, c, h, at + j]
             before = before + whole
-        row_copy(s, h).start()
-
-    def send_back(s, h):
-        view = rows_in.at[s, h]
-        pltpu.make_async_copy(view, view, row_recv.at[s, h]).wait()
+        row_copy(s, c, h).start()
+
+    def send_back(s, c, h):
+        view = rows_in.at[s, c, h]
+        pltpu.make_async_copy(view, view, row_recv.at[s, c, h]).wait()
         for j in range(WINDOW):
             passed = other < member[j] if s == 0 else other > member[j]
             passed = jnp.logical_or(passed, other_wraps)
             for r in range(NY):
                 at = (r if s == 0 else NY - 1 - r) * WINDOW + j
-                prior = rows_in[s, h, r - 1] if r else jnp.zeros((TILE, HD), F32)
-                sums[s, h, at] = sums[s, h, at] + jnp.where(passed, rows_in[s, h, r], prior)
+                prior = rows_in[s, c, h, r - 1] if r else jnp.zeros((TILE, HD), F32)
+                sums[s, c, h, at] = sums[s, c, h, at] + jnp.where(passed, rows_in[s, c, h, r], prior)
 
         def send(py, pz):
             pltpu.make_async_remote_copy(
-                src_ref=sums.at[s, h, py * WINDOW + wrap(pz - z + low + NZ, NZ)],
+                src_ref=sums.at[s, c, h, py * WINDOW + wrap(pz - z + low + NZ, NZ)],
                 dst_ref=carry.at[s, h, mine],
-                send_sem=back_send.at[s, h],
+                send_sem=back_send.at[s, c, h],
                 recv_sem=back_recv.at[s, h],
-                device_id={"ctx": py * NZ + pz},
+                device_id={"ctx": py * NZ + pz, "head": head - 1 + c},
                 device_id_type=MESH,
             ).start()
 
         each_in_window(y, z, -side(z), send)
-        pltpu.make_async_copy(
-            sums.at[s, h, y * WINDOW + low], carry.at[s, h, mine], back_recv.at[s, h]
-        ).start()
+        if c == 0:
+            send(y, z)
+        else:
+            pltpu.make_async_copy(
+                sums.at[s, c, h, y * WINDOW + low], carry.at[s, h, mine], back_recv.at[s, h]
+            ).start()
 
     def arrived(s, h):
         view = carry.at[s, h]
         pltpu.make_async_copy(view, view, back_recv.at[s, h]).wait()
 
     def add_up(s):
-        for h in range(HEADS):
-            add_window(s, h)
-        for h in range(HEADS):
-            send_back(s, h)
+        @pl.when(core == 1)
+        def _():
+            for h in range(HEADS):
+                for c in range(2):
+                    add_window(s, c, h)
+            for h in range(HEADS):
+                for c in range(2):
+                    send_back(s, c, h)
 
     def state(s, h):
         return carry[s, h].reshape(HD, HD).astype(BF16)
@@ -217,7 +232,7 @@
         kv = dot(k_ref[:, cols(h)], v_ref[:, cols(h)], 0, 0)
         own[0, h] = kv.reshape(TILES, TILE, HD)
         if h == 0:
-            pl.semaphore_wait(barrier, NEIGHBOURS + NH - 1)
+            pl.semaphore_wait(barrier, NEIGHBOURS + NH - 1 + core * (NEIGHBOURS + 1))
         send_out(0, h)
 
     for load in loads[2:]:
@@ -314,12 +329,19 @@
             stores.append(store(2 + 2 * h + i, src, dst, c))
             stores[-1].start()
 
-    for s in range(2):
-        for h in range(HEADS):
-            view = own.at[s, h, pl.ds(0, TILES - 1)]
-            pltpu.make_async_copy(view, view, out_send.at[s, h]).wait()
-            pltpu.make_async_copy(view, view, back_send.at[s, h]).wait()
-            row_copy(s, h).wait_send()
+    def drain(c):
+        for s in range(2):
+            for h in range(HEADS):
+                view = own.at[s, h, pl.ds(0, TILES - c)]
+                pltpu.make_async_copy(view, view, out_send.at[s, h]).wait()
+                if c == 1:
+                    for to in range(2):
+                        view = own.at[s, h, pl.ds(0, TILES - to)]
+                        pltpu.make_async_copy(view, view, back_send.at[s, to, h]).wait()
+                        row_copy(s, to, h).wait_send()
+
+    for c in range(2):
+        pl.when(core == c)(functools.partial(drain, c))
     pltpu.make_async_copy(seven, seven, norm_send).wait()
     for copy in stores:
         copy.wait()
@@ -363,10 +385,10 @@
             pltpu.VMEM(wide, BF16),
             pltpu.VMEM(wide, BF16),
             pltpu.VMEM((2, HEADS, TILES, TILE, HD), F32),
-            pltpu.VMEM((2, HEADS, TILES, TILE, HD), F32),
-            pltpu.VMEM((2, HEADS, NY, TILE, HD), F32),
-            pltpu.VMEM((2, HEADS, NY, TILE, HD), F32),
-            pltpu.VMEM((2, HEADS, TILES, TILE, HD), F32),
+            pltpu.VMEM((2, 2, HEADS, TILES, TILE, HD), F32),
+            pltpu.VMEM((2, 2, HEADS, NY, TILE, HD), F32),
+            pltpu.VMEM((2, 2, HEADS, NY, TILE, HD), F32),
+            pltpu.VMEM((2, 2, HEADS, TILES, TILE, HD), F32),
             pltpu.VMEM((2, HEADS, TILES, TILE, HD), F32),
             pltpu.VMEM((HEADS, ROWS, ROWS), BF16),
             pltpu.VMEM(wide, F32),
@@ -378,7 +400,9 @@
             pltpu.SemaphoreType.DMA((5,)),
             pltpu.SemaphoreType.DMA((2 + 2 * HEADS,)),
         ]
-        + [pltpu.SemaphoreType.DMA((2, HEADS))] * 6
+        + [pltpu.SemaphoreType.DMA((2, HEADS))]
+        + [pltpu.SemaphoreType.DMA((2, 2, HEADS))] * 4
+        + [pltpu.SemaphoreType.DMA((2, HEADS))]
         + [
             pltpu.SemaphoreType.DMA,
             pltpu.SemaphoreType.DMA,

time: 71.2 us -> 70.5 us (level)
  no operation moved by 1% of the time
where the time goes in v4:
time: 70.5 us; the launch traced here: 70.3 us
  Pallas kernels  69.7 us (99%)
    pallas_call x1, Pallas kernels, body(): pl.pallas_call(kernel, out_shape=(out,) * 4, in_specs=[hbm] * 5, out_spec...  67.3 us
    pallas_call x1, Pallas kernels, body(): pl.pallas_call(write_out, out_shape=(out,) * 4, in_specs=[hbm] * 4, out_s...  2.4 us

profile of v4, /device:TPU:1, one launch (start us, length us, event | category | flops | bytes accessed | tf_op | source)
XLA Modules:
  0.0 70.3 jit_solution(11533757827644822492)
XLA Ops:
  0.6 67.3 %linear_attention.1 = (bf16[512,512]{1,0:T(8,128)(2,1)}, bf16[512,512]{1,0:T(8,128)(2,1)}, bf16[512,512]{1,0:T(8,128)(2,1)}, bf16[512,512]{1,0:T(8,128)(2,1)}) custom-call(bf16[512,512]{1,0:T(8,128)(2,1)} %q_hbm.1, bf16[512,512]{1,0:T(8,128)(2,1)} %k_hbm.1, bf16[512,512]{1,0:T(8,128)(2,1)} %v_hbm.1, f32[1,512]{1,0:T(1,128)} %bitcast.1, bf16[512,512]{1,0:T(8,128)(2,1)} %g_hbm.1), custom_call_target="tpu_custom_call" | custom-call | tf_op jit(solution)/shard_map/linear_attention/pallas_call | solution.py:372
  67.9 2.4 %write_out.1 = (bf16[512,512]{1,0:T(8,128)(2,1)}, bf16[512,512]{1,0:T(8,128)(2,1)}, bf16[512,512]{1,0:T(8,128)(2,1)}, bf16[512,512]{1,0:T(8,128)(2,1)}) custom-call(bf16[512,512]{1,0:T(8,128)(2,1)} %get-tuple-element.8.a, bf16[512,512]{1,0:T(8,128)(2,1)} %get-tuple-element.9.b, bf16[512,512]{1,0:T(8,128)(2,1)} %get-tuple-element.10.c, ...), custom_call_target="tpu_custom_call" | custom-call | tf_op jit(solution)/shard_map/write_out/pallas_call | solution.py:415
